TPU v7x, 32 devices: a whole 2x2x4 slice. The times are simulated.
32 devices in a mesh: groups: 2 (over x), gx: 4 (over y, core), gy: 4 (over z).
Axes of the slice: x: 2, y: 2, z: 4, core: 2. Of those that a mesh axis runs over, the one named last changes fastest.
Arguments:
- hidden: bfloat16 [16, 16384], P('groups', 'gx'), parts along dimension 0, may hold values from -6 to 6
- norm_gain: bfloat16 [16384], P('gx'), may hold values from 0.099609375 to 1.8984375
- w_qkv: bfloat16 [16384, 9216], P('gx', 'gy'), may hold values from -0.046875 to 0.046875
- w_out: bfloat16 [8192, 16384], P('gx', 'gy'), may hold values from -0.0625 to 0.0625
- cache_keys: bfloat16 [32, 4096, 512], P(('groups', 'gx', 'gy')), parts along dimension 0, may hold values from -250 to 250
- cache_values: bfloat16 [32, 4096, 512], P(('groups', 'gx', 'gy')), parts along dimension 0, may hold values from -6 to 6
- lengths: int32 [16], P('groups'), parts along dimension 0, may hold values from 512 to 4096, as said below
- owners: int32 [16], P('groups'), parts along dimension 0, may hold values from 0 to 15, as said below
Outputs:
- output: bfloat16 [16, 16384], P(('groups', 'gx'), 'gy'), parts along dimension 0
There are 2 independent parts, one for each index of `groups`. A program takes and returns all parts, laid end to end along the dimension named above; an argument that names none is the same for every part. Nothing has to cross between parts.
Inputs may be any that keep to these rules, and one draw needn't show every extreme that they name: `lengths`: each row's cached length; some row has exactly 4096. Distinct slot numbers: row r's cache is cache_keys[owners[r]] and cache_values[owners[r]].
All inputs are finite; a program needn't handle non-finite values.
Results may differ from a plain program's by a relative error of at most 0.0075.
The roundings to bfloat16 on the way count: a program that leaves them out, or rounds other values in their place, can miss the bound.
Values may be sent and summed in bfloat16 or wider, within the bound.
A program may use at most 128 MiB of HBM per device.

v0:
```python
import jax
import jax.numpy as jnp
from jax import lax
from jax.sharding import PartitionSpec as P

D = 16384
QH = 64
KVH = 4
HD = 128


ROPE_BASE = 500000.0
EPSILON = 1e-05


def rotate(columns, position):
    half_width = columns.shape[-1] // 2
    frequency = ROPE_BASE ** (-jnp.arange(half_width, dtype=jnp.float32) * 2.0 / columns.shape[-1])
    angles = position[..., None] * frequency
    cosine = jnp.cos(angles)
    sine = jnp.sin(angles)
    first = columns[..., :half_width]
    second = columns[..., half_width:]
    return jnp.concatenate(
        [first * cosine - second * sine, first * sine + second * cosine], axis=-1
    )


def part_scores(query_grp, key_part, length):
    raw_scores = jnp.einsum(
        "ghd,tgd->ght", query_grp, key_part, preferred_element_type=jnp.float32
    ) * HD ** (-0.5)
    spots = jnp.arange(key_part.shape[0], dtype=jnp.int32)
    return jnp.where(spots[None, None, :] < length, raw_scores, -jnp.inf)


def attend_slot(query_row, key_new, value_new, key_table, value_table, length):
    groups = QH // KVH
    query_grp = query_row.reshape(KVH, groups, HD)
    own_score = jnp.einsum(
        "ghd,gd->gh", query_grp, key_new, preferred_element_type=jnp.float32
    ) * HD ** (-0.5)
    scores = part_scores(query_grp, key_table, length)
    highest = jnp.maximum(jnp.max(scores, axis=-1), own_score)
    probs = jnp.exp(scores - highest[..., None])
    summed = jnp.einsum(
        "ght,tgd->ghd", probs.astype(jnp.bfloat16), value_table, preferred_element_type=jnp.float32
    )
    total = jnp.sum(probs, axis=-1)
    own_prob = jnp.exp(own_score - highest)
    total = total + own_prob
    own_low = lax.optimization_barrier(own_prob.astype(jnp.bfloat16)).astype(jnp.float32)
    summed = summed + own_low[..., None] * value_new.astype(jnp.float32)[:, None, :]
    return (summed / total[..., None]).reshape(-1).astype(jnp.bfloat16)


def on_device(hidden, norm_gain, w_qkv, w_out, cache_keys, cache_values, lengths, owners):
    count_gx = lax.axis_size("gx")
    count_gy = lax.axis_size("gy")
    index_gx = lax.axis_index("gx")
    index_gy = lax.axis_index("gy")
    own_slot = index_gx * count_gy + index_gy
    row_block = hidden.shape[0] // count_gx
    floats = hidden.astype(jnp.float32)
    squares = lax.psum(jnp.sum(floats * floats, axis=1), "gx")
    normed = (
        floats * lax.rsqrt(squares / D + EPSILON)[:, None] * norm_gain.astype(jnp.float32)
    ).astype(jnp.bfloat16)
    projected = lax.psum_scatter(
        jnp.dot(normed, w_qkv, preferred_element_type=jnp.float32),
        "gx",
        scatter_dimension=0,
        tiled=True,
    )
    heads_here = projected.shape[1] // HD
    head_ids = index_gy * heads_here + jnp.arange(heads_here, dtype=jnp.int32)
    local_heads = projected.reshape(row_block, heads_here, HD)
    block_lengths = lax.dynamic_slice_in_dim(lengths, index_gx * row_block, row_block)
    position = block_lengths.astype(jnp.float32)[:, None]
    turned = rotate(local_heads, position)
    rotated = jnp.where((head_ids < QH + KVH)[None, :, None], turned, local_heads)
    rotated = rotated.astype(jnp.bfloat16).reshape(row_block, -1)
    full_rows = lax.all_gather(rotated, "gy", axis=1, tiled=True)
    every_row = lax.all_gather(full_rows, "gx", axis=0, tiled=True)
    picker = (owners == own_slot).astype(jnp.bfloat16)
    mine = jnp.dot(picker[None, :], every_row, preferred_element_type=jnp.float32)[0].astype(
        jnp.bfloat16
    )
    my_length = jnp.sum(jnp.where(owners == own_slot, lengths, 0))
    att_width = QH * HD
    kv_width = KVH * HD
    query_row = mine[:att_width]
    key_new = mine[att_width : att_width + kv_width].reshape(KVH, HD)
    value_new = mine[att_width + kv_width :].reshape(KVH, HD)
    key_table = cache_keys[0].reshape(-1, KVH, HD)
    value_table = cache_values[0].reshape(-1, KVH, HD)
    attended_row = attend_slot(query_row, key_new, value_new, key_table, value_table, my_length)
    att_block = att_width // count_gx
    every_output = lax.all_gather(attended_row[None, :], ("gx", "gy"), axis=0, tiled=True)
    wanted = lax.dynamic_slice_in_dim(every_output, index_gx * att_block, att_block, 1)
    slot_ids = jnp.arange(every_output.shape[0], dtype=jnp.int32)
    placer = (owners[:, None] == slot_ids[None, :]).astype(jnp.bfloat16)
    attended = jnp.dot(placer, wanted, preferred_element_type=jnp.float32).astype(jnp.bfloat16)
    return lax.psum_scatter(
        jnp.dot(attended, w_out, preferred_element_type=jnp.float32),
        "gx",
        scatter_dimension=0,
        tiled=True,
    ).astype(jnp.bfloat16)


def solution(mesh):
    in_specs = (
        P("groups", "gx"),
        P("gx"),
        P("gx", "gy"),
        P("gx", "gy"),
        P(("groups", "gx", "gy"), None, None),
        P(("groups", "gx", "gy"), None, None),
        P("groups"),
        P("groups"),
    )
    out_specs = P(("groups", "gx"), "gy")
    return jax.shard_map(
        on_device, mesh=mesh, in_specs=in_specs, out_specs=out_specs, check_vma=False
    )
```

profile of v0, /device:TPU:0, one launch (start us, length us, event | category | flops | bytes accessed | tf_op | source)
XLA Modules:
  0.0 147.1 jit_solution(15450780434559352101)
XLA Ops:
  6.5 1.0 fusion.18
  7.5 8.4 %psum.7 = f32[8]{0:T(128)S(1)} all-reduce(f32[8]{0:T(128)S(1)} %fusion.18), channel_id=1, replica_groups=mesh['groups'=2,'gx'=4,'gy'=4] {'gx'}, use_global_device_ids=true, to_apply=%region_2.0 | all-reduce | flops 8 | bytes 64 | tf_op jit(solution)/shard_map/psum | solution.py:65
  15.9 0.7 convert_element_type.59
  16.6 9.6 %fusion.21 = f32[8,2304]{1,0:T(8,128)} fusion(bf16[4096,2304]{1,0:T(8,128)(2,1)} %param.10, bf16[8,4096]{1,0:T(8,128)(2,1)} %param.8, f32[4096]{0:T(1024)S(1)} %convert_element_type.59, f32[8]{0:T(128)S(1)} %add_rsqrt_fusion), kind=kOutput, calls=%fused_computation.19 | convolution fusion | flops 151126016 | bytes 19030048 | tf_op jit(solution)/shard_map/dot_general | solution.py:70
  26.5 0.6 fusion.34
  27.2 0.7 iota_compare_fusion
  27.9 6.9 %reshape_squeeze.6 = bf16[4096,4,128]{2,1,0:T(4,128)(2,1)} reshape(bf16[1,4096,512]{2,1,0:T(8,128)(2,1)} %param.12) | data formatting | bytes 8388608 | tf_op jit(solution)/shard_map/reshape;squeeze | solution.py:95
  34.8 7.0 %reshape_squeeze.7 = bf16[4096,4,128]{2,1,0:T(4,128)(2,1)} reshape(bf16[1,4096,512]{2,1,0:T(8,128)(2,1)} %param.13) | data formatting | bytes 8388608 | tf_op jit(solution)/shard_map/reshape;squeeze | solution.py:96
  41.8 0.6 dynamic-slice.1
  43.0 13.1 %all-reduce.5.cloned.1.call-done = f32[8,2304]{1,0:T(8,128)} async-done(((f32[8,2304]{1,0:T(8,128)}), f32[8,2304]{1,0:T(8,128)}) %all-reduce.5.cloned.1.call-update) | async-done | bytes 73744
  56.1 0.9 constant_dynamic-slice_fusion
  57.1 0.9 fusion.25
  58.1 13.6 %all_gather.9 = bf16[2,9216]{1,0:T(2,128)(2,1)S(1)} all-gather(bf16[2,2304]{1,0:T(2,128)(2,1)S(1)} %fusion.25), channel_id=1, replica_groups=mesh['groups'=2,'gx'=4,'gy'=4] {'gy'}, dimensions={1}, use_global_device_ids=true | all-gather | bytes 46080 | tf_op jit(solution)/shard_map/all_gather | solution.py:83
  71.6 5.7 %all-gather = bf16[4,2,9216]{2,1,0:T(2,128)(2,1)S(1)} all-gather(bf16[1,2,9216]{2,1,0:T(2,128)(2,1)S(1)} %bitcast.36), channel_id=1, replica_groups=mesh['groups'=2,'gx'=4,'gy'=4] {'gx'}, dimensions={0}, use_global_device_ids=true | all-gather | bytes 184320 | tf_op jit(solution)/shard_map/all_gather | solution.py:84
  77.4 0.2 fusion.30
  77.6 0.1 fusion.26
  77.7 3.6 %fusion.38 = (f32[4,16]{1,0:T(4,128)S(1)}, f32[4,16,4096]{2,1,0:T(8,128)S(1)}) fusion(bf16[4,16,128]{2,1,0:T(8,128)(2,1)S(1)} %bitcast.38, bf16[4096,4,128]{2,1,0:T(4,128)(2,1)} %reshape_squeeze.6, pred[4096]{0:T(1024)(128)(4,1)S(1)} %iota_compare_fusion), kind=kOutput, calls=%fused_computation.56 | convolution fusion | flops 67895232 | bytes 5263616 | tf_op jit(solution)/shard_map/ghd,tgd->ght/dot_general | solution.py:30
  81.4 0.3 fusion.14
  81.7 0.9 fusion.11
  82.6 37.8 %all-gather.1 = bf16[16,1,8192]{2,1,0:T(2,128)(2,1)S(1)} all-gather(bf16[1,1,8192]{2,1,0:T(2,128)(2,1)S(1)} %reshape.118), channel_id=1, replica_groups=mesh['groups'=2,'gx'=4,'gy'=4] {'gx','gy'}, dimensions={0}, use_global_device_ids=true | all-gather | bytes 278528 | tf_op jit(solution)/shard_map/all_gather | solution.py:99
  120.5 0.1 constant_dynamic-slice_fusion.1
  120.6 7.1 %fusion.7 = f32[8,4096]{1,0:T(8,128)S(1)} fusion(bf16[2048,4096]{1,0:T(8,128)(2,1)} %param.11, bf16[16,1,2048]{2,1,0:T(2,128)(2,1)S(1)} %constant_dynamic-slice_fusion.1, s32[8]{0:T(128)S(1)} %copy-done.1), kind=kOutput, calls=%fused_computation.7 | convolution fusion | flops 134758528 | bytes 16973856 | tf_op jit(solution)/shard_map/dot_general | solution.py:105
  127.7 11.9 %all-reduce.6 = bf16[8,4096]{1,0:T(8,128)(2,1)S(1)} all-reduce(f32[8,4096]{1,0:T(8,128)S(1)} %fusion.7), channel_id=3, replica_groups=mesh['groups'=2,'gx'=4,'gy'=4] {'gx'}, use_global_device_ids=true, to_apply=%region_6.7.clone | all-reduce | flops 32768 | bytes 196608
  139.6 0.6 dynamic-slice_convert_fusion
  (27 shorter events, 0.6 us)
Async XLA Ops:
  6.5 49.5 %all-reduce.5.cloned.1.call-start = ((), (), s32[]{:S(2)}) async-start(), calls=%async_computation | async-start | bytes 147456
  16.6 9.8 %copy-start.2 = (s32[8]{0:T(128)S(1)}, s32[8]{0:T(128)}, u32[]{:S(2)}) copy-start(s32[8]{0:T(128)} %param.14) | copy-start | bytes 100
  16.6 9.9 %copy-start.1 = (s32[8]{0:T(128)S(1)}, s32[8]{0:T(128)}, u32[]{:S(2)}) copy-start(s32[8]{0:T(128)} %param.15) | copy-start | bytes 100
  34.8 7.0 %copy-start.3 = (u32[32]{0:T(128)S(1)}, u32[32]{0:T(128)}, u32[]{:S(2)}) copy-start(u32[32]{0:T(128)} %constant.47) | copy-start | bytes 388
  77.4 4.3 %copy-start = (bf16[4096,4,128]{2,1,0:T(4,128)(2,1)S(1)}, bf16[4096,4,128]{2,1,0:T(4,128)(2,1)}, u32[]{:S(2)}) copy-start(bf16[4096,4,128]{2,1,0:T(4,128)(2,1)} %reshape_squeeze.7) | copy-start | bytes 12582916
Sparse Core Ops, SparseCore 0:
  26.4 29.6 all-reduce.4
where the time goes:
time: 148 us; the launch traced here: 147 us
  blocking collectives  77.4 us (52%)
  matrix products  21.6 us (15%)
  local copies, waits for them, and re-layouts  16.3 us (11%)
  between operations  14.2 us (10%)
  waiting for transfers between devices  13.1 us (9%)
  other arithmetic  4.6 us (3%)
    all_gather x1, blocking collectives, on_device(): lax.all_gather(attended_row[None, :], ('gx', 'gy'), axis=0, tiled=True)  37.8 us
    all_gather x1, blocking collectives, on_device(): full_rows = lax.all_gather(rotated, 'gy', axis=1, tiled=True)  13.6 us
    unnamed x2, waiting for transfers between devices  13.1 us
    unnamed x1, blocking collectives  11.9 us
    dot_general x1, matrix products, on_device(): jnp.dot(normed, w_qkv, preferred_element_type=jnp.float32)  9.64 us
    psum x1, blocking collectives, on_device(): squares = lax.psum(jnp.sum(floats * floats, axis=1), 'gx')  8.36 us
    dot_general x1, matrix products, on_device(): jnp.dot(attended, w_out, preferred_element_type=jnp.float32)  7.12 us
    another operation x1, local copies, waits for them, and re-layouts, on_device(): value_table = cache_values[0].reshape(-1, KVH, HD)  6.95 us
  transfers between devices with their start and end apart: 1, of which 1 were waited for; matrix products, arithmetic and copies ran while one was open for 11% of the time, Pallas kernels for 0%

commit v1 on v0

v1 whole, which is shorter than its diff:
```python
import functools

import jax
import jax.numpy as jnp
import numpy as np
from jax import lax
from jax.experimental import pallas as pl
from jax.experimental.pallas import tpu as pltpu
from jax.sharding import PartitionSpec as P

D = 16384
QH = 64
KVH = 4
HD = 128
GROUP = QH // KVH
HEADS = QH + 2 * KVH

ROPE_BASE = 500000.0
EPSILON = 1e-05
MESH = pl.DeviceIdType.MESH
F32 = jnp.float32
BF16 = jnp.bfloat16


def chunks_of(heads):
    for count in (3, 2):
        if heads % count == 0:
            return count
    return 1


def kernel(
    ngx, ngy, nc, no,
    lengths, owners, freq_ref, owner_row, hidden_ref, gain_ref, w_qkv, w_out, keys, values,
    out_ref,
    wq, wo, kt, vt, x_ref, normed, sq, send1, recv1, heads, qbd, scores, send3, recv3, lhs, part, recv5,
    w_sem, kv_sem, o_sem,
    sq_send, sq_recv, s1_send, s1_recv, s3_send, s3_recv, s5_send, s5_recv,
):
    rows = hidden_ref.shape[0]
    feats = hidden_ref.shape[1]
    slots = ngx * ngy
    group = lax.axis_index("groups")
    gx = lax.axis_index("gx")
    gy = lax.axis_index("gy")
    me = gx * ngy + gy
    hpc = recv1.shape[2]
    cw = hpc * HD
    here = nc * hpc
    cap = kt.shape[0]
    hpg = recv3.shape[1]
    ow = wo.shape[2]
    block = rows // ngx

    w_copies = [
        pltpu.make_async_copy(w_qkv.at[:, pl.ds(c * cw, cw)], wq.at[c], w_sem.at[c]) for c in range(nc)
    ]
    kv_copies = [
        pltpu.make_async_copy(keys.at[0], kt, kv_sem.at[0]),
        pltpu.make_async_copy(values.at[0], vt, kv_sem.at[1]),
    ]
    o_copies = [
        pltpu.make_async_copy(w_out.at[:, pl.ds(c * ow, ow)], wo.at[c], o_sem.at[c]) for c in range(no)
    ]
    for copy in w_copies:
        copy.start()

    def peer(d):
        other = lax.rem(me + d, slots)
        return other, (group, other // ngy, lax.rem(other, ngy))

    def peer_x(d):
        other = lax.rem(gx + d, ngx)
        return other, (group, other, gy)

    barrier = pltpu.get_barrier_semaphore()

    @pl.loop(1, slots)
    def _(d):
        _, target = peer(d)
        pl.semaphore_signal(barrier, inc=1, device_id=target, device_id_type=MESH)

    picker = (
        lax.broadcasted_iota(jnp.int32, (slots, rows), 0) == jnp.broadcast_to(owner_row[...], (slots, rows))
    ).astype(BF16)
    fc = min(feats, 1024)
    total = jnp.zeros((slots, 1), F32)
    for f in range(feats // fc):
        piece = jnp.dot(picker, hidden_ref[:, f * fc : (f + 1) * fc], preferred_element_type=F32)
        x_ref[:, f * fc : (f + 1) * fc] = piece
        total = total + jnp.sum(piece * piece, axis=1, keepdims=True)
    sq[gx] = jnp.broadcast_to(total, (slots, HD))

    pl.semaphore_wait(barrier, slots - 1)

    def sq_copy(d):
        other, target = peer_x(d)
        return pltpu.make_async_remote_copy(
            src_ref=sq.at[gx], dst_ref=sq.at[gx], send_sem=sq_send.at[d], recv_sem=sq_recv.at[d],
            device_id=target, device_id_type=MESH,
        )

    for d in range(1, ngx):
        sq_copy(d).start()
    for copy in kv_copies + o_copies:
        copy.start()

    length = jnp.int32(0)
    for r in range(rows):
        length = length + jnp.where(owners[r] == me, lengths[r], 0)
    angles = length.astype(F32) * freq_ref[...]
    cosine = jnp.cos(angles)
    sine = jnp.sin(angles)
    lane = lax.broadcasted_iota(jnp.int32, (1, HD), 1)
    signed = jnp.where(lane < HD // 2, -sine, sine)

    mix_shape = (hpg * rows, slots * hpg)
    at_row = lax.broadcasted_iota(jnp.int32, (hpg * rows, 1), 0)
    at_col = lax.broadcasted_iota(jnp.int32, (1, slots * hpg), 1)
    want_row = at_row & (rows - 1)
    owner_col = jnp.zeros((hpg * rows, 1), jnp.int32)
    for r in range(rows):
        owner_col = jnp.where(want_row == r, owners[r], owner_col)
    wanted = owner_col * hpg + at_row // rows
    lhs[...] = jnp.where(
        jnp.broadcast_to(wanted, mix_shape) == jnp.broadcast_to(at_col, mix_shape), 1.0, 0.0
    ).astype(BF16)

    for d in range(1, ngx):
        sq_copy(d).wait_recv()
    squares = sq[0]
    for i in range(1, ngx):
        squares = squares + sq[i]
    scale = lax.rsqrt(squares[:, :1] / D + EPSILON)
    for f in range(feats // fc):
        at = slice(f * fc, (f + 1) * fc)
        normed[:, at] = (x_ref[:, at] * scale * gain_ref[:, at].astype(F32)).astype(BF16)

    def s1_copy(c, d):
        other, target = peer(d)
        return pltpu.make_async_remote_copy(
            src_ref=send1.at[c, other], dst_ref=recv1.at[c, me], send_sem=s1_send.at[c, d],
            recv_sem=s1_recv.at[c, d], device_id=target, device_id_type=MESH,
        )

    kc = min(feats, 512)
    for c in range(nc):
        w_copies[c].wait()

        def step(k, acc):
            at = pl.ds(pl.multiple_of(k * kc, kc), kc)
            return acc + jnp.dot(normed[:, at], wq[c, at, :], preferred_element_type=F32)

        acc = lax.fori_loop(0, feats // kc, step, jnp.zeros((slots, cw), F32))
        for h in range(hpc):
            send1[c, :, h, :] = acc[:, h * HD : (h + 1) * HD]

        @pl.loop(1, slots)
        def _(d):
            s1_copy(c, d).start()

        recv1[c, me] = send1[c, me]

    for c in range(nc):

        @pl.loop(1, slots)
        def _(d):
            s1_copy(c, d).wait_recv()

        for y in range(ngy):
            piece = recv1[c, y]
            for i in range(1, ngx):
                piece = piece + recv1[c, i * ngy + y]
            heads[pl.ds(y * here + c * hpc, hpc), :] = piece
    turning = heads[: QH + KVH, :]
    turned = (turning * cosine + pltpu.roll(turning, HD // 2, 1) * signed).astype(BF16)
    query = turned[:QH, :].astype(F32)
    qbd[...] = jnp.zeros(qbd.shape, BF16)
    own = []
    value_new = []
    for g in range(KVH):
        at = slice(g * GROUP, (g + 1) * GROUP)
        qbd[at, g * HD : (g + 1) * HD] = turned[at, :]
        key_new = turned[QH + g : QH + g + 1, :].astype(F32)
        own.append(jnp.sum(query[at, :] * key_new, axis=1, keepdims=True))
        value_new.append(heads[QH + KVH + g : QH + KVH + g + 1, :].astype(BF16).astype(F32))
    own_score = jnp.concatenate(own, axis=0) * HD ** (-0.5)

    tc = min(cap, 512)
    kv_copies[0].wait()
    q = qbd[...]
    highest = own_score
    for t in range(cap // tc):
        s = lax.dot_general(
            q, kt[t * tc : (t + 1) * tc, :], (((1,), (1,)), ((), ())), preferred_element_type=F32
        ) * HD ** (-0.5)
        spot = t * tc + lax.broadcasted_iota(jnp.int32, (1, tc), 1)
        s = jnp.where(spot < length, s, -jnp.inf)
        scores[:, t * tc : (t + 1) * tc] = s
        highest = jnp.maximum(highest, jnp.max(s, axis=1, keepdims=True))
    kv_copies[1].wait()
    own_prob = jnp.exp(own_score - highest)
    total = own_prob
    summed = jnp.zeros((QH, KVH * HD), F32)
    for t in range(cap // tc):
        p = jnp.exp(scores[:, t * tc : (t + 1) * tc] - highest)
        total = total + jnp.sum(p, axis=1, keepdims=True)
        summed = summed + jnp.dot(p.astype(BF16), vt[t * tc : (t + 1) * tc, :], preferred_element_type=F32)
    own_low = own_prob.astype(BF16).astype(F32)
    for g in range(KVH):
        at = slice(g * GROUP, (g + 1) * GROUP)
        mine = summed[at, g * HD : (g + 1) * HD] + own_low[at, :] * value_new[g]
        mine = (mine / total[at, :]).astype(send3.dtype if send3.dtype == BF16 else BF16).astype(send3.dtype)
        for i in range(GROUP // hpg):
            send3[g * (GROUP // hpg) + i] = mine[i * hpg : (i + 1) * hpg, :]

    def s3_copy(d):
        other, target = peer(d)
        return pltpu.make_async_remote_copy(
            src_ref=send3.at[other // ngy], dst_ref=recv3.at[me], send_sem=s3_send.at[d],
            recv_sem=s3_recv.at[d], device_id=target, device_id_type=MESH,
        )

    @pl.loop(1, slots)
    def _(d):
        s3_copy(d).start()

    recv3[me] = send3[gx]

    @pl.loop(1, slots)
    def _(d):
        s3_copy(d).wait_recv()

    sent = recv3[...].reshape(slots * hpg, HD).astype(BF16)
    mixed = jnp.dot(lhs[...], sent, preferred_element_type=F32)
    for h in range(hpg):
        part[:, h * HD : (h + 1) * HD] = mixed[h * rows : (h + 1) * rows, :].astype(BF16)

    def s5_copy(c, d):
        other, target = peer_x(d)
        return pltpu.make_async_remote_copy(
            src_ref=recv5.at[1, c, other], dst_ref=recv5.at[0, c, gx], send_sem=s5_send.at[c, d],
            recv_sem=s5_recv.at[c, d], device_id=target, device_id_type=MESH,
        )

    depth = wo.shape[1]
    oc = min(depth, 512)
    for c in range(no):
        o_copies[c].wait()

        def step(k, acc):
            at = pl.ds(pl.multiple_of(k * oc, oc), oc)
            return acc + jnp.dot(part[:, at], wo[c, at, :], preferred_element_type=F32)

        acc = lax.fori_loop(0, depth // oc, step, jnp.zeros((rows, ow), F32))
        for i in range(ngx):
            recv5[1, c, i] = acc[i * block : (i + 1) * block, :]
        for d in range(1, ngx):
            s5_copy(c, d).start()
        recv5[0, c, gx] = recv5[1, c, gx]
    for c in range(no):
        for d in range(1, ngx):
            s5_copy(c, d).wait_recv()
        result = recv5[0, c, 0]
        for i in range(1, ngx):
            result = result + recv5[0, c, i]
        out_ref[:, c * ow : (c + 1) * ow] = result.astype(out_ref.dtype)

    for d in range(1, ngx):
        sq_copy(d).wait_send()
        for c in range(no):
            s5_copy(c, d).wait_send()

    @pl.loop(1, slots)
    def _(d):
        s3_copy(d).wait_send()
        for c in range(nc):
            s1_copy(c, d).wait_send()


def on_device(hidden, norm_gain, w_qkv, w_out, cache_keys, cache_values, lengths, owners):
    ngx = lax.axis_size("gx")
    ngy = lax.axis_size("gy")
    slots = ngx * ngy
    rows, feats = hidden.shape
    here = w_qkv.shape[1] // HD
    nc = chunks_of(here)
    hpc = here // nc
    hpg = w_out.shape[0] // HD
    no = 4
    ow = w_out.shape[1] // no
    cap = cache_keys.shape[1]
    half = HD // 2
    freq = np.float32(ROPE_BASE) ** (-np.arange(half, dtype=np.float32) * np.float32(2.0) / np.float32(HD))
    freq = jnp.asarray(np.concatenate([freq, freq])[None, :].astype(np.float32))
    sent = BF16 if hpg % 16 == 0 else F32
    dma = pltpu.SemaphoreType.DMA
    vmem = pl.BlockSpec(memory_space=pltpu.VMEM)
    smem = pl.BlockSpec(memory_space=pltpu.SMEM)
    hbm = pl.BlockSpec(memory_space=pl.ANY)
    return pl.pallas_call(
        functools.partial(kernel, ngx, ngy, nc, no),
        out_shape=jax.ShapeDtypeStruct((rows // ngx, w_out.shape[1]), BF16),
        in_specs=[smem, smem, vmem, vmem, vmem, vmem, hbm, hbm, hbm, hbm],
        out_specs=vmem,
        scratch_shapes=[
            pltpu.VMEM((nc, feats, hpc * HD), BF16),
            pltpu.VMEM((no, w_out.shape[0], ow), BF16),
            pltpu.VMEM((cap, KVH * HD), BF16),
            pltpu.VMEM((cap, KVH * HD), BF16),
            pltpu.VMEM((slots, feats), F32),
            pltpu.VMEM((slots, feats), BF16),
            pltpu.VMEM((ngx, slots, HD), F32),
            pltpu.VMEM((nc, slots, hpc, HD), F32),
            pltpu.VMEM((nc, slots, hpc, HD), F32),
            pltpu.VMEM((HEADS, HD), F32),
            pltpu.VMEM((QH, KVH * HD), BF16),
            pltpu.VMEM((QH, cap), F32),
            pltpu.VMEM((ngx, hpg, HD), sent),
            pltpu.VMEM((slots, hpg, HD), sent),
            pltpu.VMEM((hpg * rows, slots * hpg), BF16),
            pltpu.VMEM((rows, hpg * HD), BF16),
            pltpu.VMEM((2, no, ngx, rows // ngx, ow), F32),
            dma((nc,)), dma((2,)), dma((no,)),
            dma((ngx,)), dma((ngx,)),
            dma((nc, slots)), dma((nc, slots)),
            dma((slots,)), dma((slots,)),
            dma((no, ngx)), dma((no, ngx)),
        ],
        compiler_params=pltpu.CompilerParams(
            collective_id=0, has_side_effects=True, vmem_limit_bytes=56 * 1024 * 1024
        ),
        cost_estimate=pl.CostEstimate(flops=10**9, bytes_accessed=44 * 10**6, transcendentals=0),
    )(
        lengths, owners, freq, owners[None, :], hidden, norm_gain[None, :], w_qkv, w_out,
        cache_keys, cache_values,
    )


def solution(mesh):
    in_specs = (
        P("groups", "gx"),
        P("gx"),
        P("gx", "gy"),
        P("gx", "gy"),
        P(("groups", "gx", "gy"), None, None),
        P(("groups", "gx", "gy"), None, None),
        P("groups"),
        P("groups"),
    )
    out_specs = P(("groups", "gx"), "gy")
    return jax.shard_map(
        on_device, mesh=mesh, in_specs=in_specs, out_specs=out_specs, check_vma=False
    )
```

time: 148 us -> 38.9 us (0.26)
  blocking collectives: 77.4 us -> 0 us
  Pallas kernels: 0 us -> 35.9 us
  matrix products: 21.6 us -> 0 us
  between operations: 14.2 us -> 0.01 us
  local copies, waits for them, and re-layouts: 16.3 us -> 2.65 us
  waiting for transfers between devices: 13.1 us -> 0 us
  other arithmetic: 4.6 us -> 0 us
    all_gather x3 -> x0, blocking collectives: 57.1 us -> none  [the longest x1 37.8 us: on_device(): lax.all_gather(attended_row[None, :], ('gx', 'gy'), axis=0, tiled=True)]
    pallas_call x0 -> x1, Pallas kernels: none -> 35.9 us  [on_device(): pl.pallas_call(functools.partial(kernel, ngx, ngy, nc, no), out_shape=jax...]
    dot_general x6 -> x0, matrix products: 21.6 us -> none  [the longest x1 9.64 us: on_device(): jnp.dot(normed, w_qkv, preferred_element_type=jnp.float32)]
    another operation x2 -> x0, local copies, waits for them, and re-layouts: 13.9 us -> none  [the longest x1 6.95 us: on_device(): value_table = cache_values[0].reshape(-1, KVH, HD)]
    unnamed x2 -> x0, waiting for transfers between devices: 13.1 us -> none
    unnamed x1 -> x0, blocking collectives: 11.9 us -> none
    psum x1 -> x0, blocking collectives: 8.36 us -> none  [on_device(): squares = lax.psum(jnp.sum(floats * floats, axis=1), 'gx')]
    reduce_sum x3 -> x0, other arithmetic: 1.91 us -> none  [the longest x1 0.99 us: on_device(): squares = lax.psum(jnp.sum(floats * floats, axis=1), 'gx')]
  transfers between devices with their start and end apart: 1 -> 0, of which waited for: 1 -> 0; matrix products, arithmetic and copies ran while one was open for 11% -> 0% of each run, Pallas kernels for 0% -> 0%
where the time goes in v1:
time: 38.9 us; the launch traced here: 38.6 us
  Pallas kernels  35.9 us (92%)
  local copies, waits for them, and re-layouts  2.65 us (7%)
    pallas_call x1, Pallas kernels, on_device(): pl.pallas_call(functools.partial(kernel, ngx, ngy, nc, no), out_shape=jax...  35.9 us
    unnamed x1, local copies, waits for them, and re-layouts  1.34 us
    broadcast_in_dim x1, local copies, waits for them, and re-layouts, on_device(): norm_gain[None, :]  1.31 us

profile of v1, /device:TPU:0, one launch (start us, length us, event | category | flops | bytes accessed | tf_op | source)
XLA Modules:
  0.0 38.6 jit_solution(11395097808816487942)
XLA Ops:
  0.0 1.3 %broadcast_in_dim.7.gain_ref = bf16[1,4096]{1,0:T(2,128)(2,1)} reshape(bf16[4096]{0:T(1024)(128)(2,1)} %param.10) | data formatting | bytes 16384 | tf_op jit(solution)/shard_map/broadcast_in_dim | solution.py:335
  1.3 35.9 %shard_map.91 = bf16[2,4096]{1,0:T(2,128)(2,1)} custom-call(s32[8]{0:T(128)} %lengths.1, s32[8]{0:T(128)} %owners.1, f32[1,128]{1,0:T(1,128)} %constant.2.clone.freq_ref, s32[1,8]{1,0:T(1,128)} %bitcast.1, bf16[8,4096]{1,0:T(8,128)(2,1)} %hidden_ref.1, bf16[1,4096]{1,0:T(2,128)(2,1)} %broadcast_in_dim.7.gain_ref, bf16[4096,2304]{1,0:T(8,128)(2,1)} %w_qkv.1, ...), custom_call_target="tpu_custom_call" | custom-call | flops 1000000000 | bytes 44000000 | tf_op jit(solution)/shard_map/pallas_call | solution.py:301
  37.2 1.3 %copy.11 = bf16[2,4096]{1,0:T(2,128)(2,1)} copy(bf16[2,4096]{1,0:T(2,128)(2,1)} %shard_map.91) | data formatting | bytes 32768

commit v2 on v1

--- a/solution.py
+++ b/solution.py
@@ -31,10 +31,11 @@
 
 def kernel(
     ngx, ngy, nc, no,
-    lengths, owners, freq_ref, owner_row, hidden_ref, gain_ref, w_qkv, w_out, keys, values,
+    lengths, owners, freq, hidden, gain, w_qkv, w_out, keys, values,
     out_ref,
+    freq_ref, hidden_ref, gain_ref,
     wq, wo, kt, vt, x_ref, normed, sq, send1, recv1, heads, qbd, scores, send3, recv3, lhs, part, recv5,
-    w_sem, kv_sem, o_sem,
+    in_sem, w_sem, kv_sem, o_sem,
     sq_send, sq_recv, s1_send, s1_recv, s3_send, s3_recv, s5_send, s5_recv,
 ):
     rows = hidden_ref.shape[0]
@@ -52,6 +53,11 @@
     ow = wo.shape[2]
     block = rows // ngx
 
+    hidden_copy = pltpu.make_async_copy(hidden, hidden_ref, in_sem.at[0])
+    gain_copy = pltpu.make_async_copy(gain, gain_ref, in_sem.at[1])
+    freq_copy = pltpu.make_async_copy(freq, freq_ref, in_sem.at[2])
+    for copy in (hidden_copy, gain_copy, freq_copy):
+        copy.start()
     w_copies = [
         pltpu.make_async_copy(w_qkv.at[:, pl.ds(c * cw, cw)], wq.at[c], w_sem.at[c]) for c in range(nc)
     ]
@@ -65,24 +71,47 @@
     for copy in w_copies:
         copy.start()
 
+    xs = [gx]
+    for _ in range(ngx - 1):
+        after = xs[-1] + 1
+        xs.append(jnp.where(after == ngx, 0, after))
+    ys = [gy]
+    for _ in range(ngy - 1):
+        after = ys[-1] + 1
+        ys.append(jnp.where(after == ngy, 0, after))
+
+    def peer_x(d):
+        return xs[d], (group, xs[d], gy)
+
+    few = slots <= 16
+
     def peer(d):
-        other = lax.rem(me + d, slots)
-        return other, (group, other // ngy, lax.rem(other, ngy))
-
-    def peer_x(d):
-        other = lax.rem(gx + d, ngx)
-        return other, (group, other, gy)
+        if few:
+            x, y = xs[d // ngy], ys[d % ngy]
+        else:
+            x, y = lax.rem(gx + d // ngy, ngx), lax.rem(gy + d % ngy, ngy)
+        return x * ngy + y, x, (group, x, y)
+
+    def each_peer(body):
+        if few:
+            for d in range(1, slots):
+                body(d)
+        else:
+
+            @pl.loop(1, slots)
+            def _(d):
+                body(d)
 
     barrier = pltpu.get_barrier_semaphore()
 
-    @pl.loop(1, slots)
-    def _(d):
-        _, target = peer(d)
-        pl.semaphore_signal(barrier, inc=1, device_id=target, device_id_type=MESH)
-
-    picker = (
-        lax.broadcasted_iota(jnp.int32, (slots, rows), 0) == jnp.broadcast_to(owner_row[...], (slots, rows))
-    ).astype(BF16)
+    each_peer(lambda d: pl.semaphore_signal(barrier, inc=1, device_id=peer(d)[2], device_id_type=MESH))
+
+    at_lane = lax.broadcasted_iota(jnp.int32, (slots, rows), 1)
+    owner_of = jnp.zeros((slots, rows), jnp.int32)
+    for r in range(rows):
+        owner_of = jnp.where(at_lane == r, owners[r], owner_of)
+    picker = jnp.where(lax.broadcasted_iota(jnp.int32, (slots, rows), 0) == owner_of, 1.0, 0.0).astype(BF16)
+    hidden_copy.wait()
     fc = min(feats, 1024)
     total = jnp.zeros((slots, 1), F32)
     for f in range(feats // fc):
@@ -108,6 +137,7 @@
     length = jnp.int32(0)
     for r in range(rows):
         length = length + jnp.where(owners[r] == me, lengths[r], 0)
+    freq_copy.wait()
     angles = length.astype(F32) * freq_ref[...]
     cosine = jnp.cos(angles)
     sine = jnp.sin(angles)
@@ -126,6 +156,7 @@
         jnp.broadcast_to(wanted, mix_shape) == jnp.broadcast_to(at_col, mix_shape), 1.0, 0.0
     ).astype(BF16)
 
+    gain_copy.wait()
     for d in range(1, ngx):
         sq_copy(d).wait_recv()
     squares = sq[0]
@@ -134,10 +165,10 @@
     scale = lax.rsqrt(squares[:, :1] / D + EPSILON)
     for f in range(feats // fc):
         at = slice(f * fc, (f + 1) * fc)
-        normed[:, at] = (x_ref[:, at] * scale * gain_ref[:, at].astype(F32)).astype(BF16)
+        normed[:, at] = (x_ref[:, at] * scale * jnp.broadcast_to(gain_ref[at].astype(F32), (slots, fc))).astype(BF16)
 
     def s1_copy(c, d):
-        other, target = peer(d)
+        other, _, target = peer(d)
         return pltpu.make_async_remote_copy(
             src_ref=send1.at[c, other], dst_ref=recv1.at[c, me], send_sem=s1_send.at[c, d],
             recv_sem=s1_recv.at[c, d], device_id=target, device_id_type=MESH,
@@ -155,17 +186,12 @@
         for h in range(hpc):
             send1[c, :, h, :] = acc[:, h * HD : (h + 1) * HD]
 
-        @pl.loop(1, slots)
-        def _(d):
-            s1_copy(c, d).start()
+        each_peer(lambda d: s1_copy(c, d).start())
 
         recv1[c, me] = send1[c, me]
 
     for c in range(nc):
-
-        @pl.loop(1, slots)
-        def _(d):
-            s1_copy(c, d).wait_recv()
+        each_peer(lambda d: s1_copy(c, d).wait_recv())
 
         for y in range(ngy):
             piece = recv1[c, y]
@@ -210,29 +236,25 @@
     for g in range(KVH):
         at = slice(g * GROUP, (g + 1) * GROUP)
         mine = summed[at, g * HD : (g + 1) * HD] + own_low[at, :] * value_new[g]
-        mine = (mine / total[at, :]).astype(send3.dtype if send3.dtype == BF16 else BF16).astype(send3.dtype)
+        mine = (mine / total[at, :]).astype(BF16).astype(send3.dtype)
         for i in range(GROUP // hpg):
             send3[g * (GROUP // hpg) + i] = mine[i * hpg : (i + 1) * hpg, :]
 
     def s3_copy(d):
-        other, target = peer(d)
+        _, x, target = peer(d)
         return pltpu.make_async_remote_copy(
-            src_ref=send3.at[other // ngy], dst_ref=recv3.at[me], send_sem=s3_send.at[d],
+            src_ref=send3.at[x], dst_ref=recv3.at[me], send_sem=s3_send.at[d],
             recv_sem=s3_recv.at[d], device_id=target, device_id_type=MESH,
         )
 
-    @pl.loop(1, slots)
-    def _(d):
-        s3_copy(d).start()
+    each_peer(lambda d: s3_copy(d).start())
 
     recv3[me] = send3[gx]
 
-    @pl.loop(1, slots)
-    def _(d):
-        s3_copy(d).wait_recv()
-
-    sent = recv3[...].reshape(slots * hpg, HD).astype(BF16)
-    mixed = jnp.dot(lhs[...], sent, preferred_element_type=F32)
+    each_peer(lambda d: s3_copy(d).wait_recv())
+
+    groups = recv3[...].reshape(slots * hpg, HD).astype(BF16)
+    mixed = jnp.dot(lhs[...], groups, preferred_element_type=F32)
     for h in range(hpg):
         part[:, h * HD : (h + 1) * HD] = mixed[h * rows : (h + 1) * rows, :].astype(BF16)
 
@@ -271,11 +293,12 @@
         for c in range(no):
             s5_copy(c, d).wait_send()
 
-    @pl.loop(1, slots)
-    def _(d):
+    def sent(d):
         s3_copy(d).wait_send()
         for c in range(nc):
             s1_copy(c, d).wait_send()
+
+    each_peer(sent)
 
 
 def on_device(hidden, norm_gain, w_qkv, w_out, cache_keys, cache_values, lengths, owners):
@@ -301,9 +324,12 @@
     return pl.pallas_call(
         functools.partial(kernel, ngx, ngy, nc, no),
         out_shape=jax.ShapeDtypeStruct((rows // ngx, w_out.shape[1]), BF16),
-        in_specs=[smem, smem, vmem, vmem, vmem, vmem, hbm, hbm, hbm, hbm],
+        in_specs=[smem, smem, hbm, hbm, hbm, hbm, hbm, hbm, hbm],
         out_specs=vmem,
         scratch_shapes=[
+            pltpu.VMEM((1, HD), F32),
+            pltpu.VMEM((rows, feats), BF16),
+            pltpu.VMEM((feats,), BF16),
             pltpu.VMEM((nc, feats, hpc * HD), BF16),
             pltpu.VMEM((no, w_out.shape[0], ow), BF16),
             pltpu.VMEM((cap, KVH * HD), BF16),
@@ -321,7 +347,7 @@
             pltpu.VMEM((hpg * rows, slots * hpg), BF16),
             pltpu.VMEM((rows, hpg * HD), BF16),
             pltpu.VMEM((2, no, ngx, rows // ngx, ow), F32),
-            dma((nc,)), dma((2,)), dma((no,)),
+            dma((3,)), dma((nc,)), dma((2,)), dma((no,)),
             dma((ngx,)), dma((ngx,)),
             dma((nc, slots)), dma((nc, slots)),
             dma((slots,)), dma((slots,)),
@@ -332,7 +358,7 @@
         ),
         cost_estimate=pl.CostEstimate(flops=10**9, bytes_accessed=44 * 10**6, transcendentals=0),
     )(
-        lengths, owners, freq, owners[None, :], hidden, norm_gain[None, :], w_qkv, w_out,
+        lengths, owners, freq, hidden, norm_gain, w_qkv, w_out,
         cache_keys, cache_values,
     )
 

time: 38.9 us -> 36.9 us (0.949)
  local copies, waits for them, and re-layouts: 2.65 us -> 1.34 us
  Pallas kernels: 35.9 us -> 35.3 us
    broadcast_in_dim x1 -> x0, local copies, waits for them, and re-layouts: 1.31 us -> none  [on_device(): norm_gain[None, :]]
    pallas_call x1, Pallas kernels: 35.9 us -> 35.3 us  [on_device(): pl.pallas_call(functools.partial(kernel, ngx, ngy, nc, no), out_shape=jax...]
where the time goes in v2:
time: 36.9 us; the launch traced here: 36.6 us
  Pallas kernels  35.3 us (96%)
  local copies, waits for them, and re-layouts  1.34 us (4%)
    pallas_call x1, Pallas kernels, on_device(): pl.pallas_call(functools.partial(kernel, ngx, ngy, nc, no), out_shape=jax...  35.3 us
    unnamed x1, local copies, waits for them, and re-layouts  1.34 us

profile of v2, /device:TPU:0, one launch (start us, length us, event | category | flops | bytes accessed | tf_op | source)
XLA Modules:
  0.0 36.6 jit_solution(11040050343902302912)
XLA Ops:
  0.0 35.3 %shard_map.91 = bf16[2,4096]{1,0:T(2,128)(2,1)} custom-call(s32[8]{0:T(128)} %lengths.1, s32[8]{0:T(128)} %owners.1, f32[1,128]{1,0:T(1,128)} %constant.2.clone.freq, bf16[8,4096]{1,0:T(8,128)(2,1)} %hidden.1, bf16[4096]{0:T(1024)(128)(2,1)} %gain.1, bf16[4096,2304]{1,0:T(8,128)(2,1)} %w_qkv.1, bf16[2048,4096]{1,0:T(8,128)(2,1)} %w_out.1, ...), custom_call_target="tpu_custom_call" | custom-call | flops 1000000000 | bytes 44000000 | tf_op jit(solution)/shard_map/pallas_call | solution.py:324
  35.3 1.3 %copy.11 = bf16[2,4096]{1,0:T(2,128)(2,1)} copy(bf16[2,4096]{1,0:T(2,128)(2,1)} %shard_map.91) | data formatting | bytes 32768

commit v3 on v2

--- a/solution.py
+++ b/solution.py
@@ -20,13 +20,6 @@
 MESH = pl.DeviceIdType.MESH
 F32 = jnp.float32
 BF16 = jnp.bfloat16
-
-
-def chunks_of(heads):
-    for count in (3, 2):
-        if heads % count == 0:
-            return count
-    return 1
 
 
 def kernel(
@@ -80,6 +73,10 @@
         after = ys[-1] + 1
         ys.append(jnp.where(after == ngy, 0, after))
 
+    def all_of(ref, count, semaphore):
+        some = ref.at[pl.ds(0, count)]
+        pltpu.make_async_copy(some, some, semaphore).wait()
+
     def peer_x(d):
         return xs[d], (group, xs[d], gy)
 
@@ -125,7 +122,7 @@
     def sq_copy(d):
         other, target = peer_x(d)
         return pltpu.make_async_remote_copy(
-            src_ref=sq.at[gx], dst_ref=sq.at[gx], send_sem=sq_send.at[d], recv_sem=sq_recv.at[d],
+            src_ref=sq.at[gx], dst_ref=sq.at[gx], send_sem=sq_send, recv_sem=sq_recv,
             device_id=target, device_id_type=MESH,
         )
 
@@ -157,8 +154,7 @@
     ).astype(BF16)
 
     gain_copy.wait()
-    for d in range(1, ngx):
-        sq_copy(d).wait_recv()
+    all_of(sq, ngx - 1, sq_recv)
     squares = sq[0]
     for i in range(1, ngx):
         squares = squares + sq[i]
@@ -170,8 +166,8 @@
     def s1_copy(c, d):
         other, _, target = peer(d)
         return pltpu.make_async_remote_copy(
-            src_ref=send1.at[c, other], dst_ref=recv1.at[c, me], send_sem=s1_send.at[c, d],
-            recv_sem=s1_recv.at[c, d], device_id=target, device_id_type=MESH,
+            src_ref=send1.at[c, other], dst_ref=recv1.at[c, me], send_sem=s1_send.at[c],
+            recv_sem=s1_recv.at[c], device_id=target, device_id_type=MESH,
         )
 
     kc = min(feats, 512)
@@ -191,7 +187,7 @@
         recv1[c, me] = send1[c, me]
 
     for c in range(nc):
-        each_peer(lambda d: s1_copy(c, d).wait_recv())
+        all_of(recv1.at[c], slots - 1, s1_recv.at[c])
 
         for y in range(ngy):
             piece = recv1[c, y]
@@ -243,15 +239,18 @@
     def s3_copy(d):
         _, x, target = peer(d)
         return pltpu.make_async_remote_copy(
-            src_ref=send3.at[x], dst_ref=recv3.at[me], send_sem=s3_send.at[d],
-            recv_sem=s3_recv.at[d], device_id=target, device_id_type=MESH,
+            src_ref=send3.at[x], dst_ref=recv3.at[me], send_sem=s3_send,
+            recv_sem=s3_recv, device_id=target, device_id_type=MESH,
         )
 
     each_peer(lambda d: s3_copy(d).start())
 
     recv3[me] = send3[gx]
 
-    each_peer(lambda d: s3_copy(d).wait_recv())
+    all_of(sq, ngx - 1, sq_send)
+    for c in range(nc):
+        all_of(send1.at[c], slots - 1, s1_send.at[c])
+    all_of(recv3, slots - 1, s3_recv)
 
     groups = recv3[...].reshape(slots * hpg, HD).astype(BF16)
     mixed = jnp.dot(lhs[...], groups, preferred_element_type=F32)
@@ -261,8 +260,8 @@
     def s5_copy(c, d):
         other, target = peer_x(d)
         return pltpu.make_async_remote_copy(
-            src_ref=recv5.at[1, c, other], dst_ref=recv5.at[0, c, gx], send_sem=s5_send.at[c, d],
-            recv_sem=s5_recv.at[c, d], device_id=target, device_id_type=MESH,
+            src_ref=recv5.at[1, c, other], dst_ref=recv5.at[0, c, gx], send_sem=s5_send.at[c],
+            recv_sem=s5_recv.at[c], device_id=target, device_id_type=MESH,
         )
 
     depth = wo.shape[1]
@@ -281,24 +280,16 @@
             s5_copy(c, d).start()
         recv5[0, c, gx] = recv5[1, c, gx]
     for c in range(no):
-        for d in range(1, ngx):
-            s5_copy(c, d).wait_recv()
+        if c == 0:
+            all_of(recv3, slots - 1, s3_send)
+        all_of(recv5.at[0, c], ngx - 1, s5_recv.at[c])
         result = recv5[0, c, 0]
         for i in range(1, ngx):
             result = result + recv5[0, c, i]
         out_ref[:, c * ow : (c + 1) * ow] = result.astype(out_ref.dtype)
 
-    for d in range(1, ngx):
-        sq_copy(d).wait_send()
-        for c in range(no):
-            s5_copy(c, d).wait_send()
-
-    def sent(d):
-        s3_copy(d).wait_send()
-        for c in range(nc):
-            s1_copy(c, d).wait_send()
-
-    each_peer(sent)
+    for c in range(no):
+        all_of(recv5.at[0, c], ngx - 1, s5_send.at[c])
 
 
 def on_device(hidden, norm_gain, w_qkv, w_out, cache_keys, cache_values, lengths, owners):
@@ -307,10 +298,10 @@
     slots = ngx * ngy
     rows, feats = hidden.shape
     here = w_qkv.shape[1] // HD
-    nc = chunks_of(here)
+    nc = 1
     hpc = here // nc
     hpg = w_out.shape[0] // HD
-    no = 4
+    no = 1
     ow = w_out.shape[1] // no
     cap = cache_keys.shape[1]
     half = HD // 2
@@ -348,10 +339,10 @@
             pltpu.VMEM((rows, hpg * HD), BF16),
             pltpu.VMEM((2, no, ngx, rows // ngx, ow), F32),
             dma((3,)), dma((nc,)), dma((2,)), dma((no,)),
-            dma((ngx,)), dma((ngx,)),
-            dma((nc, slots)), dma((nc, slots)),
-            dma((slots,)), dma((slots,)),
-            dma((no, ngx)), dma((no, ngx)),
+            dma, dma,
+            dma((nc,)), dma((nc,)),
+            dma, dma,
+            dma((no,)), dma((no,)),
         ],
         compiler_params=pltpu.CompilerParams(
             collective_id=0, has_side_effects=True, vmem_limit_bytes=56 * 1024 * 1024

time: 36.9 us -> 33.5 us (0.908)
  Pallas kernels: 35.3 us -> 31.9 us
    pallas_call x1, Pallas kernels: 35.3 us -> 31.9 us  [on_device(): pl.pallas_call(functools.partial(kernel, ngx, ngy, nc, no), out_shape=jax...]
where the time goes in v3:
time: 33.5 us; the launch traced here: 33.3 us
  Pallas kernels  31.9 us (95%)
  local copies, waits for them, and re-layouts  1.34 us (4%)
    pallas_call x1, Pallas kernels, on_device(): pl.pallas_call(functools.partial(kernel, ngx, ngy, nc, no), out_shape=jax...  31.9 us
    unnamed x1, local copies, waits for them, and re-layouts  1.34 us

profile of v3, /device:TPU:0, one launch (start us, length us, event | category | flops | bytes accessed | tf_op | source)
XLA Modules:
  0.0 33.3 jit_solution(5689344361758816089)
XLA Ops:
  0.0 31.9 %shard_map.91 = bf16[2,4096]{1,0:T(2,128)(2,1)} custom-call(s32[8]{0:T(128)} %lengths.1, s32[8]{0:T(128)} %owners.1, f32[1,128]{1,0:T(1,128)} %constant.2.clone.freq, bf16[8,4096]{1,0:T(8,128)(2,1)} %hidden.1, bf16[4096]{0:T(1024)(128)(2,1)} %gain.1, bf16[4096,2304]{1,0:T(8,128)(2,1)} %w_qkv.1, bf16[2048,4096]{1,0:T(8,128)(2,1)} %w_out.1, ...), custom_call_target="tpu_custom_call" | custom-call | flops 1000000000 | bytes 44000000 | tf_op jit(solution)/shard_map/pallas_call | solution.py:315
  31.9 1.3 %copy.11 = bf16[2,4096]{1,0:T(2,128)(2,1)} copy(bf16[2,4096]{1,0:T(2,128)(2,1)} %shard_map.91) | data formatting | bytes 32768

commit v4 on v3

--- a/solution.py
+++ b/solution.py
@@ -91,7 +91,7 @@
 
     def each_peer(body):
         if few:
-            for d in range(1, slots):
+            for d in sorted(range(1, slots), key=lambda d: -(d % ngy) * ngx - d // ngy):
                 body(d)
         else:
 
@@ -178,7 +178,7 @@
             at = pl.ds(pl.multiple_of(k * kc, kc), kc)
             return acc + jnp.dot(normed[:, at], wq[c, at, :], preferred_element_type=F32)
 
-        acc = lax.fori_loop(0, feats // kc, step, jnp.zeros((slots, cw), F32))
+        acc = lax.fori_loop(0, feats // kc, step, jnp.zeros((slots, cw), F32), unroll=True)
         for h in range(hpc):
             send1[c, :, h, :] = acc[:, h * HD : (h + 1) * HD]
 
@@ -273,7 +273,7 @@
             at = pl.ds(pl.multiple_of(k * oc, oc), oc)
             return acc + jnp.dot(part[:, at], wo[c, at, :], preferred_element_type=F32)
 
-        acc = lax.fori_loop(0, depth // oc, step, jnp.zeros((rows, ow), F32))
+        acc = lax.fori_loop(0, depth // oc, step, jnp.zeros((rows, ow), F32), unroll=True)
         for i in range(ngx):
             recv5[1, c, i] = acc[i * block : (i + 1) * block, :]
         for d in range(1, ngx):

time: 33.5 us -> 32.3 us (0.964)
  Pallas kernels: 31.9 us -> 30.7 us
    pallas_call x1, Pallas kernels: 31.9 us -> 30.7 us  [on_device(): pl.pallas_call(functools.partial(kernel, ngx, ngy, nc, no), out_shape=jax...]
where the time goes in v4:
time: 32.3 us; the launch traced here: 32 us
  Pallas kernels  30.7 us (95%)
  local copies, waits for them, and re-layouts  1.34 us (4%)
    pallas_call x1, Pallas kernels, on_device(): pl.pallas_call(functools.partial(kernel, ngx, ngy, nc, no), out_shape=jax...  30.7 us
    unnamed x1, local copies, waits for them, and re-layouts  1.34 us

profile of v4, /device:TPU:0, one launch (start us, length us, event | category | flops | bytes accessed | tf_op | source)
XLA Modules:
  0.0 32.0 jit_solution(9318406519331204590)
XLA Ops:
  0.0 30.7 %shard_map.91 = bf16[2,4096]{1,0:T(2,128)(2,1)} custom-call(s32[8]{0:T(128)} %lengths.1, s32[8]{0:T(128)} %owners.1, f32[1,128]{1,0:T(1,128)} %constant.2.clone.freq, bf16[8,4096]{1,0:T(8,128)(2,1)} %hidden.1, bf16[4096]{0:T(1024)(128)(2,1)} %gain.1, bf16[4096,2304]{1,0:T(8,128)(2,1)} %w_qkv.1, bf16[2048,4096]{1,0:T(8,128)(2,1)} %w_out.1, ...), custom_call_target="tpu_custom_call" | custom-call | flops 1000000000 | bytes 44000000 | tf_op jit(solution)/shard_map/pallas_call | solution.py:315
  30.7 1.3 %copy.11 = bf16[2,4096]{1,0:T(2,128)(2,1)} copy(bf16[2,4096]{1,0:T(2,128)(2,1)} %shard_map.91) | data formatting | bytes 32768

commit v5 on v4

--- a/solution.py
+++ b/solution.py
@@ -298,7 +298,7 @@
     slots = ngx * ngy
     rows, feats = hidden.shape
     here = w_qkv.shape[1] // HD
-    nc = 1
+    nc = 2 if here % 2 == 0 else 1
     hpc = here // nc
     hpg = w_out.shape[0] // HD
     no = 1

time: 32.3 us -> 31 us (0.960)
  Pallas kernels: 30.7 us -> 29.4 us
    pallas_call x1, Pallas kernels: 30.7 us -> 29.4 us  [on_device(): pl.pallas_call(functools.partial(kernel, ngx, ngy, nc, no), out_shape=jax...]
where the time goes in v5:
time: 31 us; the launch traced here: 30.7 us
  Pallas kernels  29.4 us (95%)
  local copies, waits for them, and re-layouts  1.34 us (4%)
    pallas_call x1, Pallas kernels, on_device(): pl.pallas_call(functools.partial(kernel, ngx, ngy, nc, no), out_shape=jax...  29.4 us
    unnamed x1, local copies, waits for them, and re-layouts  1.34 us

profile of v5, /device:TPU:0, one launch (start us, length us, event | category | flops | bytes accessed | tf_op | source)
XLA Modules:
  0.0 30.7 jit_solution(10320430568108045087)
XLA Ops:
  0.0 29.4 %shard_map.91 = bf16[2,4096]{1,0:T(2,128)(2,1)} custom-call(s32[8]{0:T(128)} %lengths.1, s32[8]{0:T(128)} %owners.1, f32[1,128]{1,0:T(1,128)} %constant.2.clone.freq, bf16[8,4096]{1,0:T(8,128)(2,1)} %hidden.1, bf16[4096]{0:T(1024)(128)(2,1)} %gain.1, bf16[4096,2304]{1,0:T(8,128)(2,1)} %w_qkv.1, bf16[2048,4096]{1,0:T(8,128)(2,1)} %w_out.1, ...), custom_call_target="tpu_custom_call" | custom-call | flops 1000000000 | bytes 44000000 | tf_op jit(solution)/shard_map/pallas_call | solution.py:315
  29.4 1.3 %copy.11 = bf16[2,4096]{1,0:T(2,128)(2,1)} copy(bf16[2,4096]{1,0:T(2,128)(2,1)} %shard_map.91) | data formatting | bytes 32768
